TPU v7x, 32 devices: a whole 2x2x4 slice. The times are simulated.
32 devices in a mesh: layer: 4 (over x, core), row: 8 (over z, y).
Axes of the slice: x: 2, y: 2, z: 4, core: 2. Of those that a mesh axis runs over, the one named last changes fastest.
Arguments:
- conc: float32 [2, 128, 256, 512], P(None, 'layer', 'row'), may hold values from -10 to 10
- explicit_rate: bfloat16 [2, 128, 256, 512], P(None, 'layer', 'row'), may hold values from 0.029907227 to 0.23925781
- x_coef: bfloat16 [2, 128, 256, 512], P(None, 'layer', 'row'), may hold values from 4 to 400
- y_coef: bfloat16 [2, 128, 256, 512], P(None, 'layer', 'row'), may hold values from 300 to 5984
- z_inverse: bfloat16 [16, 128, 256, 512], P(None, 'layer', 'row'), may hold values from 0.13964844 to 0.6015625
- z_link: float32 [2, 8, 256, 512], P(None, 'layer', 'row'), may hold values from 0.5 to 1
Outputs:
- new_conc: float32 [2, 128, 256, 512], P(None, 'layer', 'row')
All inputs are finite; a program needn't handle non-finite values.
Results may differ from a plain program's by a relative error of at most 0.0003.
Values sent between devices are 32-bit elements; how exact they have to be, the bound alone decides.
A program may use at most 384 MiB of HBM per device.

v0:
```python
import jax
import jax.numpy as jnp
from jax import lax
from jax.sharding import PartitionSpec as P


def with_halo(shard, sides, width):
    for axis, dim in sides:
        devices, length = (lax.axis_size(axis), shard.shape[dim])
        up = [(i, (i + 1) % devices) for i in range(devices - 1)]
        down = [(j, i) for i, j in up]
        last = lax.slice_in_dim(shard, length - width, length, axis=dim)
        first = lax.slice_in_dim(shard, 0, width, axis=dim)
        before = lax.ppermute(last, axis, up)
        after = lax.ppermute(first, axis, down)
        shard = jnp.concatenate([before, shard, after], axis=dim)
    return shard


def shifted(values, stride, line_axis, forward):
    line_axis = line_axis % values.ndim
    length = values.shape[line_axis]
    widths = [(0, 0)] * values.ndim
    if forward:
        retained = lax.slice_in_dim(values, 0, length - stride, axis=line_axis)
        widths[line_axis] = (stride, 0)
    else:
        retained = lax.slice_in_dim(values, stride, length, axis=line_axis)
        widths[line_axis] = (0, stride)
    return jnp.pad(retained, widths)


def cyclic_reduce(lower_band, upper_band, right_side, line_axis):
    length = lower_band.shape[line_axis % lower_band.ndim]
    stride = 1
    while stride < length:
        lower_before = shifted(lower_band, stride, line_axis, True)
        upper_before = shifted(upper_band, stride, line_axis, True)
        lower_after = shifted(lower_band, stride, line_axis, False)
        upper_after = shifted(upper_band, stride, line_axis, False)
        right_before = shifted(right_side, stride, line_axis, True)
        right_after = shifted(right_side, stride, line_axis, False)
        factor = 1.0 / (1.0 - lower_band * upper_before - upper_band * lower_after)
        right_side = (right_side + lower_band * right_before + upper_band * right_after) * factor
        lower_band, upper_band = (
            lower_band * lower_before * factor,
            upper_band * upper_after * factor,
        )
        stride = stride * 2
    return right_side


def normalized(coefficient, values):
    toward_low = coefficient[0].astype(jnp.float32)
    toward_high = coefficient[1].astype(jnp.float32)
    inverse_diag = 1.0 / (1.0 + toward_low + toward_high)
    return (toward_low * inverse_diag, toward_high * inverse_diag, values * inverse_diag)


def interface_solve(top_value, bottom_value, top_low, bottom_low, top_high, bottom_high):

    def forward(state_pair, entries):
        offset_part, slope_part = state_pair
        head_value, tail_value, head_low, tail_low, head_high, tail_high = entries
        factor = 1.0 / (1.0 - head_low * slope_part)
        base_part = (head_value + head_low * offset_part) * factor
        gain_part = head_high * factor
        next_offset = tail_value + tail_low * offset_part + tail_low * slope_part * base_part
        next_slope = tail_high + tail_low * slope_part * gain_part
        return ((next_offset, next_slope), (base_part, gain_part, offset_part, slope_part))

    initial = (jnp.zeros_like(top_value[0]), jnp.zeros_like(top_low[0]))
    _, stored = lax.scan(
        forward, initial, (top_value, bottom_value, top_low, bottom_low, top_high, bottom_high)
    )

    def backward(top_later, entries):
        base_part, gain_part, offset_part, slope_part = entries
        top_here = base_part + gain_part * top_later
        bottom_before = offset_part + slope_part * top_here
        return (top_here, (bottom_before, top_later))

    _, (bottom_before, top_after) = lax.scan(
        backward, jnp.zeros_like(top_value[0]), stored, reverse=True
    )
    return (bottom_before, top_after)


def vertical_pieces(values, inverse, link):
    block_size = inverse.shape[0]
    block_count = values.shape[1] // block_size
    grouped = values.reshape(
        values.shape[0], block_count, block_size, values.shape[2], values.shape[3]
    )
    inverse_blocks = inverse.reshape(
        block_size, block_count, block_size, inverse.shape[2], inverse.shape[3]
    )
    local_part = None
    for column in range(block_size):
        product_term = (
            inverse_blocks[column].astype(jnp.float32)[None] * grouped[:, :, column : column + 1]
        )
        local_part = product_term if column == 0 else local_part + product_term
    low_spike = link[0][:, None] * inverse_blocks[0].astype(jnp.float32)
    high_spike = link[1][:, None] * inverse_blocks[block_size - 1].astype(jnp.float32)
    return (local_part, low_spike, high_spike)


def local(conc, explicit_rate, x_coef, y_coef, z_inverse, z_link):
    species = conc.shape[0]
    padded = with_halo(conc, (("layer", 1), ("row", 2)), 1)
    rate_pair = explicit_rate.astype(jnp.float32)
    center = padded[:, 1:-1, 1:-1]
    across_rows = padded[:, 1:-1, :-2] + padded[:, 1:-1, 2:] - 2.0 * center
    across_layers = padded[:, :-2, 1:-1] + padded[:, 2:, 1:-1] - 2.0 * center
    explicit = center + rate_pair[0] * across_rows + rate_pair[1] * across_layers
    low_band, high_band, scaled = normalized(x_coef, explicit)
    first_pass = cyclic_reduce(low_band, high_band, scaled, -1)
    low_band, high_band, scaled = normalized(y_coef, first_pass)
    row_count = conc.shape[2]
    row_index = lax.broadcasted_iota(jnp.int32, low_band.shape, 1)
    spike_low = jnp.where(row_index == 0, low_band, 0.0)
    spike_high = jnp.where(row_index == row_count - 1, high_band, 0.0)
    stacked = jnp.concatenate([scaled, spike_low[None], spike_high[None]], 0)
    solved = cyclic_reduce(low_band, high_band, stacked, -2)
    local_rows = solved[:species]
    low_rows = solved[species]
    high_rows = solved[species + 1]
    end_values = jnp.concatenate(
        [
            local_rows[:, :, 0],
            local_rows[:, :, row_count - 1],
            low_rows[None, :, 0],
            low_rows[None, :, row_count - 1],
            high_rows[None, :, 0],
            high_rows[None, :, row_count - 1],
        ],
        0,
    )
    everyone = lax.all_gather(end_values[None], "row", axis=0, tiled=True)
    bottom_rows, top_rows = interface_solve(
        everyone[:, :species],
        everyone[:, species : 2 * species],
        everyone[:, 2 * species],
        everyone[:, 2 * species + 1],
        everyone[:, 2 * species + 2],
        everyone[:, 2 * species + 3],
    )
    position = lax.axis_index("row")
    bottom_mine = lax.dynamic_index_in_dim(bottom_rows, position, 0, keepdims=False)
    top_mine = lax.dynamic_index_in_dim(top_rows, position, 0, keepdims=False)
    middle = (
        local_rows
        + low_rows[None] * bottom_mine[:, :, None]
        + high_rows[None] * top_mine[:, :, None]
    )
    local_part, low_spike, high_spike = vertical_pieces(middle, z_inverse, z_link)
    final_row = low_spike.shape[1] - 1
    end_blocks = jnp.concatenate(
        [
            jnp.moveaxis(local_part[:, :, 0], 1, 0),
            jnp.moveaxis(local_part[:, :, final_row], 1, 0),
            low_spike[:, 0:1],
            low_spike[:, final_row : final_row + 1],
            high_spike[:, 0:1],
            high_spike[:, final_row : final_row + 1],
        ],
        1,
    )
    all_blocks = lax.all_gather(end_blocks, "layer", axis=0, tiled=True)
    bottom_before, top_after = interface_solve(
        all_blocks[:, :species],
        all_blocks[:, species : 2 * species],
        all_blocks[:, 2 * species],
        all_blocks[:, 2 * species + 1],
        all_blocks[:, 2 * species + 2],
        all_blocks[:, 2 * species + 3],
    )
    block_count = low_spike.shape[0]
    first_block = lax.axis_index("layer") * block_count
    bottom_mine = lax.dynamic_slice_in_dim(bottom_before, first_block, block_count, 0)
    top_mine = lax.dynamic_slice_in_dim(top_after, first_block, block_count, 0)
    result = (
        local_part
        + low_spike[None] * jnp.moveaxis(bottom_mine, 0, 1)[:, :, None]
        + high_spike[None] * jnp.moveaxis(top_mine, 0, 1)[:, :, None]
    )
    return result.reshape(conc.shape)


def solution(mesh):
    placed = (
        P(None, "layer", "row", None),
        P(None, "layer", "row", None),
        P(None, "layer", "row", None),
        P(None, "layer", "row", None),
        P(None, "layer", "row", None),
        P(None, "layer", "row", None),
    )
    return jax.shard_map(
        local, mesh=mesh, in_specs=placed, out_specs=P(None, "layer", "row", None), check_vma=False
    )
```

profile of v0, /device:TPU:0, one launch (start us, length us, event | category | flops | bytes accessed | tf_op | source)
XLA Modules:
  0.0 658.3 jit_solution(15161007629996813667)
XLA Ops:
  96.9 5.5 fusion.28
  109.8 4.3 collective-permute-start.2
  122.6 5.4 fusion.9
  128.1 4.9 fusion.78
  132.9 17.2 %add_multiply_fusion.12 = f32[2,32,32,512]{3,1,2,0:T(8,128)} fusion(f32[2,32,32,511]{3,1,2,0:T(8,128)} %get-tuple-element.898, f32[2,32,32,511]{3,1,2,0:T(8,128)} %get-tuple-element.897, f32[32,32,512]{2,0,1:T(8,128)} %copy-done.47, f32[32,32,512]{2,0,1:T(8,128)} %get-tuple-element.957, f32[32,32,512]{2,0,1:T(8,128)} %get-tuple-element.956, ...), kind=kLoop, calls=%fused_computation.75 | loop fusion | flops 24117248 | bytes 29884416 | tf_op jit(solution)/shard_map/mul | solution.py:44
  150.1 7.0 %fusion.77 = (f32[2,32,32,510]{3,1,2,0:T(8,128)S(1)}, f32[2,32,32,510]{3,1,2,0:T(8,128)}) fusion(f32[2,32,32,512]{3,1,2,0:T(8,128)} %add_multiply_fusion.12), kind=kLoop, calls=%fused_computation.260 | loop fusion | bytes 16711680 | tf_op jit(solution)/shard_map/slice | solution.py:25
  165.1 4.2 add_multiply_fusion.10
  173.2 4.6 add_multiply_fusion.9
  181.7 4.2 add_multiply_fusion.8
  189.7 4.2 add_multiply_fusion.7
  211.0 4.3 fusion.66
  215.2 9.8 %add_multiply_fusion.4 = f32[4,32,32,512]{3,1,2,0:T(8,128)} fusion(f32[4,32,31,512]{3,1,2,0:T(8,128)} %get-tuple-element.850, f32[4,32,31,512]{3,1,2,0:T(8,128)S(1)} %get-tuple-element.849, f32[32,32,512]{2,0,1:T(8,128)S(1)} %copy-done.59, f32[32,32,512]{2,0,1:T(8,128)} %get-tuple-element.919, f32[32,32,512]{2,0,1:T(8,128)} %get-tuple-element.917, ...), kind=kLoop, calls=%fused_computation.45 | loop fusion | flops 14680064 | bytes 39321600 | tf_op jit(solution)/shard_map/mul | solution.py:44
  225.0 14.9 %fusion.65 = (f32[4,32,30,512]{3,1,2,0:T(8,128)}, f32[4,32,30,512]{3,1,2,0:T(8,128)}) fusion(f32[4,32,32,512]{3,1,2,0:T(8,128)} %add_multiply_fusion.4), kind=kLoop, calls=%fused_computation.248 | loop fusion | bytes 31457280 | tf_op jit(solution)/shard_map/slice | solution.py:25
  239.9 14.9 %add_multiply_fusion.3 = f32[4,32,32,512]{3,1,2,0:T(8,128)} fusion(f32[4,32,30,512]{3,1,2,0:T(8,128)} %get-tuple-element.848, f32[4,32,32,512]{3,1,2,0:T(8,128)} %add_multiply_fusion.4, f32[4,32,30,512]{3,1,2,0:T(8,128)} %get-tuple-element.847, f32[32,32,512]{2,0,1:T(8,128)} %copy-done.51, f32[32,32,512]{2,0,1:T(8,128)S(1)} %copy-done.11, ...), kind=kLoop, calls=%fused_computation.44 | loop fusion | flops 10485760 | bytes 38797312 | tf_op jit(solution)/shard_map/mul | solution.py:44
  254.8 14.0 %fusion.64 = (f32[4,32,28,512]{3,1,2,0:T(8,128)}, f32[4,32,28,512]{3,1,2,0:T(8,128)}) fusion(f32[4,32,32,512]{3,1,2,0:T(8,128)} %add_multiply_fusion.3), kind=kLoop, calls=%fused_computation.247 | loop fusion | bytes 29360128 | tf_op jit(solution)/shard_map/slice | solution.py:25
  268.8 14.7 %add_multiply_fusion.2 = f32[4,32,32,512]{3,1,2,0:T(8,128)} fusion(f32[4,32,28,512]{3,1,2,0:T(8,128)} %get-tuple-element.846, f32[4,32,32,512]{3,1,2,0:T(8,128)} %add_multiply_fusion.3, f32[4,32,28,512]{3,1,2,0:T(8,128)} %get-tuple-element.845, f32[32,32,512]{2,0,1:T(8,128)} %copy-done.60, f32[32,32,512]{2,0,1:T(8,128)S(1)} %copy-done.13, ...), kind=kLoop, calls=%fused_computation.43 | loop fusion | flops 10485760 | bytes 37748736 | tf_op jit(solution)/shard_map/mul | solution.py:44
  283.6 12.2 %fusion.63 = (f32[4,32,24,512]{3,1,2,0:T(8,128)}, f32[4,32,24,512]{3,1,2,0:T(8,128)}) fusion(f32[4,32,32,512]{3,1,2,0:T(8,128)} %add_multiply_fusion.2), kind=kLoop, calls=%fused_computation.246 | loop fusion | bytes 25165824 | tf_op jit(solution)/shard_map/slice | solution.py:25
  295.8 8.8 %add_multiply_fusion.1 = f32[4,32,32,512]{3,1,2,0:T(8,128)S(1)} fusion(f32[4,32,24,512]{3,1,2,0:T(8,128)} %get-tuple-element.844, f32[4,32,32,512]{3,1,2,0:T(8,128)} %add_multiply_fusion.2, f32[4,32,24,512]{3,1,2,0:T(8,128)} %get-tuple-element.843, f32[32,32,512]{2,0,1:T(8,128)S(1)} %copy-done.53, f32[32,32,512]{2,0,1:T(8,128)S(1)} %copy-done.17, ...), kind=kLoop, calls=%fused_computation.42 | loop fusion | flops 10485760 | bytes 35651584 | tf_op jit(solution)/shard_map/mul | solution.py:44
  304.6 4.7 fusion.62
  309.4 7.2 %add_multiply_fusion = f32[4,32,32,512]{3,1,2,0:T(8,128)} fusion(f32[4,32,16,512]{3,1,2,0:T(8,128)} %get-tuple-element.842, f32[4,32,32,512]{3,1,2,0:T(8,128)S(1)} %add_multiply_fusion.1, f32[4,32,16,512]{3,1,2,0:T(8,128)} %get-tuple-element.841, f32[32,32,512]{2,0,1:T(8,128)S(1)} %copy-done.86, f32[32,32,512]{2,0,1:T(8,128)S(1)} %copy-done.46, ...), kind=kLoop, calls=%fused_computation.41 | loop fusion | flops 10485760 | bytes 31457280 | tf_op jit(solution)/shard_map/mul | solution.py:44
  323.3 12.2 %slice_convert_fusion.15 = (f32[1,32,32,512]{3,2,1,0:T(8,128)S(1)}, f32[1,32,32,512]{3,2,1,0:T(8,128)}, f32[1,32,32,512]{3,2,1,0:T(8,128)}, f32[1,32,32,512]{3,2...) fusion(bf16[16,32,32,512]{3,2,1,0:T(8,128)(2,1)} %param.18), kind=kLoop, calls=%fused_computation.167 | loop fusion | flops 6815744 | bytes 40894464 | tf_op jit(solution)/shard_map/convert_element_type | solution.py:101
  339.4 17.4 %fusion.32 = (f32[32,32,512]{2,1,0:T(8,128)}, f32[32,32,512]{2,1,0:T(8,128)}, f32[32,32,512]{2,1,0:T(8,128)}, f32[32,32,512]{2,1,0:T(8,128)}, f32[32,32,512]{2,1...) fusion(bf16[16,32,32,512]{3,2,1,0:T(8,128)(2,1)} %param.18), kind=kLoop, calls=%fused_computation.176 | loop fusion | flops 8388608 | bytes 56623104 | tf_op jit(solution)/shard_map/convert_element_type | solution.py:101
  356.8 41.9 %all-gather.6.cloned.1.call-done = f32[64,32,512]{2,1,0:T(8,128)} async-done(((f32[8,32,512]{2,1,0:T(8,128)}), f32[64,32,512]{2,1,0:T(8,128)}) %all-gather.6.cloned.1.call-update) | async-done | bytes 4194320 | tf_op jit(solution)/shard_map/all_gather | solution.py:140
  407.1 34.2 %while.80 = (s32[]{:T(128)}, f32[2,32,512]{2,1,0:T(8,128)S(1)}, f32[32,512]{1,0:T(8,128)S(1)}, f32[8,2,32,512]{3,2,1,0:T(8,128)}, f32[8,32,512]{2,1,0:T(8,128)},...) while((s32[]{:T(128)}, f32[2,32,512]{2,1,0:T(8,128)S(1)}, ...), condition=%wide.region_1.2_spmd.clone, body=%wide.region_0.1_spmd.clone.sunk | while | flops 557059 | bytes 2426018 | solution.py:73
  442.5 20.9 %while.81 = (s32[]{:T(128)}, f32[2,32,512]{2,1,0:T(8,128)S(1)}, f32[8,2,32,512]{3,2,1,0:T(8,128)S(1)}, f32[8,2,32,512]{3,2,1,0:T(8,128)}, f32[8,2,32,512]{3,2,1,...) while((s32[]{:T(128)}, f32[2,32,512]{2,1,0:T(8,128)S(1)}, ...), condition=%wide.region_3.4_spmd.clone, body=%wide.region_2.3_spmd.clone.sunk | while | flops 163844 | bytes 1179787 | solution.py:83
  464.3 4.5 fusion.4
  481.0 13.4 %multiply_add_fusion.1 = f32[2,2,16,32,512]{4,3,1,0,2:T(8,128)S(1)} fusion(f32[2,2,32,512]{3,2,1,0:T(8,128)S(1)} %bitcast.505, f32[2,2,32,512]{3,2,1,0:T(8,128)S(1)} %bitcast.507, f32[2,2,32,512]{3,2,1,0:T(8,128)S(1)} %bitcast.509, f32[2,2,32,512]{3,2,1,0:T(8,128)S(1)} %bitcast.511, f32[2,2,32,512]{3,2,1,0:T(8,128)S(1)} %bitcast.513, ...), kind=kLoop, calls=%fused_computation.66 | loop fusion | flops 32505856 | bytes 41943040 | tf_op jit(solution)/shard_map/add | solution.py:103
  499.4 4.2 bitcast_multiply_fusion.3
  503.6 28.7 %all-gather.4.cloned.1.call-done = f32[8,8,32,512]{3,2,0,1:T(8,128)} async-done(((f32[2,8,32,512]{3,2,0,1:T(8,128)}), f32[8,8,32,512]{3,2,0,1:T(8,128)}) %all-gather.4.cloned.1.call-update) | async-done | bytes 4194320 | tf_op jit(solution)/shard_map/all_gather | solution.py:170
  538.5 28.7 %while.82 = (s32[]{:T(128)}, f32[2,32,512]{2,1,0:T(8,128)S(1)}, f32[32,512]{1,0:T(8,128)S(1)}, f32[8,2,32,512]{3,2,1,0:T(8,128)S(1)}, f32[8,32,512]{2,1,0:T(8,12...) while((s32[]{:T(128)}, f32[2,32,512]{2,1,0:T(8,128)S(1)}, ...), condition=%wide.region_5.6_spmd.clone, body=%wide.region_4.5_spmd.clone.sunk | while | flops 557059 | bytes 2425510 | solution.py:73
  568.4 13.3 %while.83 = (s32[]{:T(128)}, f32[2,32,512]{2,1,0:T(8,128)S(1)}, f32[8,2,32,512]{3,2,1,0:T(8,128)S(1)}, f32[8,2,32,512]{3,2,1,0:T(8,128)}, f32[8,2,32,512]{3,2,1,...) while((s32[]{:T(128)}, f32[2,32,512]{2,1,0:T(8,128)S(1)}, ...), condition=%wide.region_7.8_spmd.clone, body=%wide.region_6.7_spmd.clone.sunk | while | flops 163844 | bytes 1179787 | solution.py:83
  619.9 31.4 %multiply_add_fusion = f32[2,32,32,512]{3,2,1,0:T(8,128)} fusion(f32[2,32,32,512]{3,2,1,0:T(8,128)S(1)} %bitcast.471, f32[2,32,32,512]{3,2,1,0:T(8,128)S(1)} %bitcast.470, f32[2,32,32,512]{3,2,1,0:T(8,128)} %bitcast.487, f32[2,32,32,512]{3,2,1,0:T(8,128)} %bitcast.486, f32[2,32,32,512]{3,2,1,0:T(8,128)} %bitcast.485, f32[2,32,32,512]{3,2,1,0:T(8,128)} %bitcast.484, ...), kind=kLoop, calls=%fused_computation.65 | loop fusion | flops 36700160 | bytes 117440512 | tf_op jit(solution)/shard_map/add | solution.py:184
  (527 shorter events, 321.4 us)
Async XLA Ops:
  6.5 392.2 %all-gather.6.cloned.1.call-start = ((), (), s32[]{:S(2)}) async-start(), calls=%async_computation.1 | async-start | bytes 4718592 | tf_op jit(solution)/shard_map/all_gather | solution.py:140
  8.3 100.7 %collective-permute-start = (f32[2,1,32,512]{3,1,2,0:T(1,128)}, f32[2,1,32,512]{3,1,2,0:T(1,128)}, u32[]{:S(2)}, u32[]{:S(2)}) collective-permute-start(f32[2,1,32,512]{3,1,2,0:T(1,128)} %copy.134), channel_id=1, source_target_pairs={{0,8},{8,16},{16,24},{1,9},{9,17},{17,25},{2,10},{10,18},{18,26},{... | collective-permute-start | bytes 393224 | tf_op jit(solution)/shard_map/ppermute | solution.py:14
  12.1 96.9 %collective-permute-start.1 = (f32[2,1,32,512]{3,1,2,0:T(1,128)}, f32[2,1,32,512]{3,1,2,0:T(1,128)}, u32[]{:S(2)}, u32[]{:S(2)}) collective-permute-start(f32[2,1,32,512]{3,1,2,0:T(1,128)} %copy.135), channel_id=1, source_target_pairs={{8,0},{16,8},{24,16},{9,1},{17,9},{25,17},{10,2},{18,10},{26,18},{... | collective-permute-start | bytes 393224 | tf_op jit(solution)/shard_map/ppermute | solution.py:15
  30.4 60.1 %copy-start.42 = (f32[32,32,512]{2,0,1:T(8,128)}, f32[32,32,512]{2,0,1:T(8,128)S(1)}, u32[]{:S(2)}) copy-start(f32[32,32,512]{2,0,1:T(8,128)S(1)} %get-tuple-element.769) | copy-start | bytes 6291460
  105.9 16.7 %copy-start.50 = (f32[32,32,512]{2,0,1:T(8,128)}, f32[32,32,512]{2,0,1:T(8,128)S(1)}, u32[]{:S(2)}) copy-start(f32[32,32,512]{2,0,1:T(8,128)S(1)} %get-tuple-element.958) | copy-start | bytes 6291460
  108.4 14.2 %copy-start.14 = (f32[2,32,32,512]{3,1,2,0:T(8,128)}, f32[2,32,32,512]{3,1,2,0:T(8,128)S(1)}, u32[]{:S(2)}) copy-start(f32[2,32,32,512]{3,1,2,0:T(8,128)S(1)} %copy.138) | copy-start | bytes 12582916
  109.8 8.6 %collective-permute-start.2 = (f32[2,34,1,512]{3,1,2,0:T(8,128)S(1)}, f32[2,34,1,512]{3,1,2,0:T(8,128)S(1)}, u32[]{:S(2)}, u32[]{:S(2)}) collective-permute-start(f32[2,34,1,512]{3,1,2,0:T(8,128)S(1)} %get-tuple-element.851), channel_id=1, source_target_pairs={{0,1},{1,2},{2,3},{3,4},{4,5},{5,6},{6,7},{8,9},{9,10},{10,11},{11... | collective-permute-start | bytes 417800 | tf_op jit(solution)/shard_map/ppermute | solution.py:14
  114.1 8.5 %collective-permute-start.3 = (f32[2,34,1,512]{3,1,2,0:T(8,128)S(1)}, f32[2,34,1,512]{3,1,2,0:T(8,128)S(1)}, u32[]{:S(2)}, u32[]{:S(2)}) collective-permute-start(f32[2,34,1,512]{3,1,2,0:T(8,128)S(1)} %get-tuple-element.852), channel_id=1, source_target_pairs={{1,0},{2,1},{3,2},{4,3},{5,4},{6,5},{7,6},{9,8},{10,9},{11,10},{12... | collective-permute-start | bytes 417800 | tf_op jit(solution)/shard_map/ppermute | solution.py:15
  118.4 9.6 %copy-start.49 = (f32[32,32,512]{2,0,1:T(8,128)}, f32[32,32,512]{2,0,1:T(8,128)S(1)}, u32[]{:S(2)}) copy-start(f32[32,32,512]{2,0,1:T(8,128)S(1)} %copy.139) | copy-start | bytes 6291460
  225.0 14.9 %copy-start.11 = (f32[32,32,512]{2,0,1:T(8,128)S(1)}, f32[32,32,512]{2,0,1:T(8,128)}, u32[]{:S(2)}) copy-start(f32[32,32,512]{2,0,1:T(8,128)} %copy-done.10) | copy-start | bytes 6291460
  254.8 14.0 %copy-start.13 = (f32[32,32,512]{2,0,1:T(8,128)S(1)}, f32[32,32,512]{2,0,1:T(8,128)}, u32[]{:S(2)}) copy-start(f32[32,32,512]{2,0,1:T(8,128)} %copy-done.12) | copy-start | bytes 6291460
  283.5 12.2 %copy-start.17 = (f32[32,32,512]{2,0,1:T(8,128)S(1)}, f32[32,32,512]{2,0,1:T(8,128)}, u32[]{:S(2)}) copy-start(f32[32,32,512]{2,0,1:T(8,128)} %copy-done.16) | copy-start | bytes 6291460
  283.5 12.2 %copy-start.37 = (f32[32,32,512]{2,0,1:T(8,128)S(1)}, f32[32,32,512]{2,0,1:T(8,128)}, u32[]{:S(2)}) copy-start(f32[32,32,512]{2,0,1:T(8,128)} %copy-done.36) | copy-start | bytes 6291460
  283.5 12.2 %copy-start.53 = (f32[32,32,512]{2,0,1:T(8,128)S(1)}, f32[32,32,512]{2,0,1:T(8,128)}, u32[]{:S(2)}) copy-start(f32[32,32,512]{2,0,1:T(8,128)} %copy-done.52) | copy-start | bytes 6291460
  323.2 209.1 %all-gather.4.cloned.1.call-start = ((), (), s32[]{:S(2)}) async-start(), calls=%async_computation | async-start | bytes 5242880 | tf_op jit(solution)/shard_map/all_gather | solution.py:170
  323.3 12.2 %copy-start.125 = (f32[2,32,512]{2,1,0:T(8,128)}, f32[2,32,512]{2,1,0:T(8,128)S(1)}, u32[]{:S(2)}) copy-start(f32[2,32,512]{2,1,0:T(8,128)S(1)} %get-tuple-element.967) | copy-start | bytes 393220
  323.3 12.2 %copy-start.127 = (f32[2,32,512]{2,1,0:T(8,128)}, f32[2,32,512]{2,1,0:T(8,128)S(1)}, u32[]{:S(2)}) copy-start(f32[2,32,512]{2,1,0:T(8,128)S(1)} %get-tuple-element.968) | copy-start | bytes 393220
  468.9 12.1 %copy-start.80 = (f32[1,32,32,512]{3,2,1,0:T(8,128)S(1)}, f32[1,32,32,512]{3,2,1,0:T(8,128)}, u32[]{:S(2)}) copy-start(f32[1,32,32,512]{3,2,1,0:T(8,128)} %get-tuple-element.827) | copy-start | bytes 6291460
  468.9 12.1 %copy-start.81 = (f32[1,32,32,512]{3,2,1,0:T(8,128)S(1)}, f32[1,32,32,512]{3,2,1,0:T(8,128)}, u32[]{:S(2)}) copy-start(f32[1,32,32,512]{3,2,1,0:T(8,128)} %get-tuple-element.828) | copy-start | bytes 6291460
  468.9 12.1 %copy-start.82 = (f32[1,32,32,512]{3,2,1,0:T(8,128)S(1)}, f32[1,32,32,512]{3,2,1,0:T(8,128)}, u32[]{:S(2)}) copy-start(f32[1,32,32,512]{3,2,1,0:T(8,128)} %get-tuple-element.829) | copy-start | bytes 6291460
  468.9 12.1 %copy-start.83 = (f32[1,32,32,512]{3,2,1,0:T(8,128)S(1)}, f32[1,32,32,512]{3,2,1,0:T(8,128)}, u32[]{:S(2)}) copy-start(f32[1,32,32,512]{3,2,1,0:T(8,128)} %get-tuple-element.830) | copy-start | bytes 6291460
  472.6 8.4 %copy-start.79 = (f32[1,32,32,512]{3,2,1,0:T(8,128)S(1)}, f32[1,32,32,512]{3,2,1,0:T(8,128)}, u32[]{:S(2)}) copy-start(f32[1,32,32,512]{3,2,1,0:T(8,128)} %get-tuple-element.823) | copy-start | bytes 6291460
  472.7 8.2 %copy-start.90 = (f32[2,2,1,32,512]{4,3,1,0,2:T(8,128)}, f32[2,2,1,32,512]{4,3,1,0,2:T(8,128)S(1)}, u32[]{:S(2)}) copy-start(f32[2,2,1,32,512]{4,3,1,0,2:T(8,128)S(1)} %copy.390) | copy-start | bytes 786436
  472.8 8.1 %copy-start.92 = (f32[2,2,1,32,512]{4,3,1,0,2:T(8,128)}, f32[2,2,1,32,512]{4,3,1,0,2:T(8,128)S(1)}, u32[]{:S(2)}) copy-start(f32[2,2,1,32,512]{4,3,1,0,2:T(8,128)S(1)} %copy.391) | copy-start | bytes 786436
  478.0 16.4 %copy-start.106 = (f32[2,2,1,32,512]{4,3,1,0,2:T(8,128)}, f32[2,2,1,32,512]{4,3,1,0,2:T(8,128)S(1)}, u32[]{:S(2)}) copy-start(f32[2,2,1,32,512]{4,3,1,0,2:T(8,128)S(1)} %copy.398) | copy-start | bytes 786436
  479.4 15.0 %copy-start.108 = (f32[2,2,1,32,512]{4,3,1,0,2:T(8,128)}, f32[2,2,1,32,512]{4,3,1,0,2:T(8,128)S(1)}, u32[]{:S(2)}) copy-start(f32[2,2,1,32,512]{4,3,1,0,2:T(8,128)S(1)} %copy.399) | copy-start | bytes 786436
  480.5 13.9 %copy-start.110 = (f32[2,2,1,32,512]{4,3,1,0,2:T(8,128)}, f32[2,2,1,32,512]{4,3,1,0,2:T(8,128)S(1)}, u32[]{:S(2)}) copy-start(f32[2,2,1,32,512]{4,3,1,0,2:T(8,128)S(1)} %copy.400) | copy-start | bytes 786436
  480.6 13.9 %copy-start.112 = (f32[2,2,1,32,512]{4,3,1,0,2:T(8,128)}, f32[2,2,1,32,512]{4,3,1,0,2:T(8,128)S(1)}, u32[]{:S(2)}) copy-start(f32[2,2,1,32,512]{4,3,1,0,2:T(8,128)S(1)} %copy.401) | copy-start | bytes 786436
  480.7 13.8 %copy-start.114 = (f32[2,2,1,32,512]{4,3,1,0,2:T(8,128)}, f32[2,2,1,32,512]{4,3,1,0,2:T(8,128)S(1)}, u32[]{:S(2)}) copy-start(f32[2,2,1,32,512]{4,3,1,0,2:T(8,128)S(1)} %copy.402) | copy-start | bytes 786436
  480.7 13.8 %copy-start.116 = (f32[2,2,1,32,512]{4,3,1,0,2:T(8,128)}, f32[2,2,1,32,512]{4,3,1,0,2:T(8,128)S(1)}, u32[]{:S(2)}) copy-start(f32[2,2,1,32,512]{4,3,1,0,2:T(8,128)S(1)} %copy.403) | copy-start | bytes 786436
  480.8 13.7 %copy-start.118 = (f32[2,2,1,32,512]{4,3,1,0,2:T(8,128)}, f32[2,2,1,32,512]{4,3,1,0,2:T(8,128)S(1)}, u32[]{:S(2)}) copy-start(f32[2,2,1,32,512]{4,3,1,0,2:T(8,128)S(1)} %copy.404) | copy-start | bytes 786436
  480.9 13.7 %copy-start.120 = (f32[2,2,1,32,512]{4,3,1,0,2:T(8,128)}, f32[2,2,1,32,512]{4,3,1,0,2:T(8,128)S(1)}, u32[]{:S(2)}) copy-start(f32[2,2,1,32,512]{4,3,1,0,2:T(8,128)S(1)} %copy.405) | copy-start | bytes 786436
  (106 other events, 370.0 us)
Sparse Core Ops, SparseCore 0:
  323.3 75.3 all-gather.5
  499.5 32.7 all-gather.3
where the time goes:
time: 671 us; the launch traced here: 658 us
  other arithmetic  335 us (50%)
  local copies, waits for them, and re-layouts  222 us (33%)
  waiting for transfers between devices  74.8 us (11%)
  between operations  15.8 us (2%)
  starting transfers between devices  9.89 us (1%)
    mul x13, other arithmetic, cyclic_reduce(): (right_side + lower_band * right_before + upper_band * right_after) * factor  98.2 us
    slice x17, local copies, waits for them, and re-layouts, shifted(): retained = lax.slice_in_dim(values, 0, length - stride, axis=line_axis)  80.7 us
    dynamic_update_slice x48, other arithmetic, interface_solve(): lax.scan(forward, initial, (top_value, bottom_value, top_low, bottom_low,...  50.5 us
    mul x32, local copies, waits for them, and re-layouts, vertical_pieces(): inverse_blocks[column].astype(jnp.float32)[None]  42.3 us
    all_gather x1, waiting for transfers between devices, local(): everyone = lax.all_gather(end_values[None], 'row', axis=0, tiled=True)  41.9 us
    add x1, other arithmetic, local(): local_part + low_spike[None] * jnp.moveaxis(bottom_mine, 0, 1)[:, :, None]  31.4 us
    convert_element_type x2, other arithmetic, vertical_pieces(): inverse_blocks[column].astype(jnp.float32)[None]  29.6 us
    all_gather x1, waiting for transfers between devices, local(): all_blocks = lax.all_gather(end_blocks, 'layer', axis=0, tiled=True)  28.7 us
  transfers between devices with their start and end apart: 6, of which 3 were waited for; matrix products, arithmetic and copies ran while one was open for 19% of the time, Pallas kernels for 0%

commit v1 on v0

v1 whole, which is shorter than its diff:
```python
import functools

import jax
import jax.numpy as jnp
from jax import lax
from jax.experimental import pallas as pl
from jax.experimental.pallas import tpu as pltpu
from jax.sharding import PartitionSpec as P

F32 = jnp.float32
LANES = 128
SUB = 8


def neighbours(shard, axis, dim):
    devices, length = lax.axis_size(axis), shard.shape[dim]
    up = [(i, i + 1) for i in range(devices - 1)]
    down = [(j, i) for i, j in up]
    last = lax.slice_in_dim(shard, length - 1, length, axis=dim)
    first = lax.slice_in_dim(shard, 0, 1, axis=dim)
    return lax.ppermute(last, axis, up), lax.ppermute(first, axis, down)


def horizontal_kernel(
    conc, zlo, zhi, ylo, yhi, rate, xc, yc,
    solved, low_out, high_out, ends,
    lo_s, hi_s, rhs, ya, yb,
):
    species, nz, ny, nx = conc.shape
    blocks = nx // LANES
    per = LANES // ny
    groups = nz // per
    row = lax.broadcasted_iota(jnp.int32, (ny, nx), 0)

    def explicit_of(s, z):
        here = conc[s, z]
        before = jnp.where(row == 0, ylo[s, z], pltpu.roll(here, 1, 0))
        after = jnp.where(row == ny - 1, yhi[s, z], pltpu.roll(here, ny - 1, 0))
        below = zlo[s, 0] if z == 0 else conc[s, z - 1]
        above = zhi[s, 0] if z == nz - 1 else conc[s, z + 1]
        r0 = rate[0, z].astype(F32)
        r1 = rate[1, z].astype(F32)
        two = 2.0 * here
        return here + r0 * (before + after - two) + r1 * (below + above - two)

    def put(ref, g, tall):
        for q in range(blocks):
            ref[pl.ds(q * LANES * SUB + g, LANES, stride=SUB), :] = tall[
                :, q * LANES : (q + 1) * LANES
            ].T

    for g in range(groups):
        zs = range(g * per, (g + 1) * per)
        for s in range(species):
            put(rhs.at[s], g, jnp.concatenate([explicit_of(s, z) for z in zs], 0))
        put(lo_s, g, jnp.concatenate([xc[0, z].astype(F32) for z in zs], 0))
        put(hi_s, g, jnp.concatenate([xc[1, z].astype(F32) for z in zs], 0))

    half = nx // 2
    zero = jnp.zeros((SUB, LANES), F32)
    one = jnp.ones((SUB, LANES), F32)

    def at(i):
        return pl.ds(pl.multiple_of(i * SUB, SUB), SUB)

    def forward(i, state):
        gl, gr, fl, fr, _, _ = state
        j = nx - 1 - i
        a, b = lo_s[at(i), :], hi_s[at(i), :]
        e = 1.0 + a * gl
        r = 1.0 / (e + b)
        cl = b * r
        gl = e * r
        fl = tuple((rhs[s, at(i), :] + a * fl[s]) * r for s in range(species))
        hi_s[at(i), :] = cl
        a, b = lo_s[at(j), :], hi_s[at(j), :]
        e = 1.0 + b * gr
        r = 1.0 / (e + a)
        cr = a * r
        gr = e * r
        fr = tuple((rhs[s, at(j), :] + b * fr[s]) * r for s in range(species))
        lo_s[at(j), :] = cr
        for s in range(species):
            rhs[s, at(i), :] = fl[s]
            rhs[s, at(j), :] = fr[s]
        return gl, gr, fl, fr, cl, cr

    start = (one, one, (zero,) * species, (zero,) * species, zero, zero)
    gl, gr, fl, fr, cl, cr = lax.fori_loop(0, half, forward, start, unroll=4)
    meet = 1.0 / (gl + cl * gr)
    ul = tuple((fl[s] + cl * fr[s]) * meet for s in range(species))
    ur = tuple((fr[s] + cr * fl[s]) * meet for s in range(species))
    for s in range(species):
        rhs[s, at(half - 1), :] = ul[s]
        rhs[s, at(half), :] = ur[s]

    def backward(t, state):
        ul, ur = state
        i = half - 2 - t
        j = half + 1 + t
        cl = hi_s[at(i), :]
        cr = lo_s[at(j), :]
        ul = tuple(rhs[s, at(i), :] + cl * ul[s] for s in range(species))
        ur = tuple(rhs[s, at(j), :] + cr * ur[s] for s in range(species))
        for s in range(species):
            rhs[s, at(i), :] = ul[s]
            rhs[s, at(j), :] = ur[s]
        return ul, ur

    lax.fori_loop(0, half - 1, backward, (ul, ur), unroll=5)

    for g in range(groups):
        for q in range(blocks):
            for s in range(species):
                wide = rhs[s, pl.ds(q * LANES * SUB + g, LANES, stride=SUB), :].T
                for p in range(per):
                    solved[s, q, pl.ds(g * per + p, ny, stride=nz), :] = wide[
                        p * ny : (p + 1) * ny
                    ]
    for z in range(nz):
        a, b = yc[0, z].astype(F32), yc[1, z].astype(F32)
        for q in range(blocks):
            cols = slice(q * LANES, (q + 1) * LANES)
            ya[q, pl.ds(z, ny, stride=nz), :] = a[:, cols]
            yb[q, pl.ds(z, ny, stride=nz), :] = b[:, cols]

    def line(q, _):
        tile = (nz, LANES)
        g = jnp.ones(tile, F32)
        f = [jnp.zeros(tile, F32) for _ in range(species)]
        spike = jnp.ones(tile, F32)
        for y in range(ny):
            rows = pl.ds(y * nz, nz)
            a, b = ya[q, rows, :], yb[q, rows, :]
            e = 1.0 + a * g
            r = 1.0 / (e + b)
            g = e * r
            ar = a * r
            c = b * r
            f = [solved[s, q, rows, :] * r + ar * f[s] for s in range(species)]
            spike = ar * spike
            for s in range(species):
                solved[s, q, rows, :] = f[s]
            low_out[q, rows, :] = spike
            high_out[q, rows, :] = c
        for s in range(species):
            ends[species + s, q] = f[s]
        ends[2 * species + 1, q] = spike
        ends[2 * species + 3, q] = c
        high = c
        low = spike
        for y in range(ny - 2, -1, -1):
            rows = pl.ds(y * nz, nz)
            c = high_out[q, rows, :]
            f = [solved[s, q, rows, :] + c * f[s] for s in range(species)]
            low = low_out[q, rows, :] + c * low
            high = c * high
            for s in range(species):
                solved[s, q, rows, :] = f[s]
            low_out[q, rows, :] = low
            high_out[q, rows, :] = high
        for s in range(species):
            ends[s, q] = f[s]
        ends[2 * species, q] = low
        ends[2 * species + 2, q] = high
        return 0

    lax.fori_loop(0, blocks, line, 0)


def horizontal(conc, rate, x_coef, y_coef):
    species, nz, ny, nx = conc.shape
    blocks = nx // LANES
    zlo, zhi = neighbours(conc, "layer", 1)
    ylo, yhi = neighbours(conc, "row", 2)
    flat = (blocks, ny * nz, LANES)
    shape = lambda *dims: jax.ShapeDtypeStruct(dims, F32)
    vmem = pl.BlockSpec(memory_space=pltpu.VMEM)
    return pl.pallas_call(
        horizontal_kernel,
        out_shape=(
            shape(species, *flat),
            shape(*flat),
            shape(*flat),
            shape(2 * species + 4, blocks, nz, LANES),
        ),
        in_specs=[vmem] * 8,
        out_specs=(vmem,) * 4,
        scratch_shapes=[
            pltpu.VMEM((nx * SUB, LANES), F32),
            pltpu.VMEM((nx * SUB, LANES), F32),
            pltpu.VMEM((species, nx * SUB, LANES), F32),
            pltpu.VMEM(flat, F32),
            pltpu.VMEM(flat, F32),
        ],
        compiler_params=pltpu.CompilerParams(vmem_limit_bytes=50 * 1024 * 1024),
        name="horizontal",
    )(conc, zlo, zhi, ylo, yhi, rate, x_coef, y_coef)


def vertical_kernel(solved, low, high, before, after, inverse, link, part, ends, mid):
    species, width = solved.shape[0], solved.shape[1]
    ny = solved.shape[2]
    size = inverse.shape[0]
    for q in range(width):
        for y in range(ny):
            lo, hi = low[q, y], high[q, y]
            for s in range(species):
                value = solved[s, q, y] + lo * before[s, q] + hi * after[s, q]
                mid[s, q, pl.ds(y, size, stride=ny), :] = value

    for q in range(width):
        cols = slice(q * LANES, (q + 1) * LANES)

        def layer(z, _):
            total = [None] * species
            for j in range(size):
                v = inverse[j, z, :, cols].astype(F32)
                for s in range(species):
                    term = v * mid[s, q, j * ny : (j + 1) * ny, :]
                    total[s] = term if j == 0 else total[s] + term
            for s in range(species):
                part[s, z, :, cols] = total[s]
            return 0

        lax.fori_loop(0, size, layer, 0)
        l0, l1 = link[0, 0, :, cols], link[1, 0, :, cols]
        for e, z in enumerate((0, size - 1)):
            for s in range(species):
                ends[0, e * species + s, :, cols] = part[s, z, :, cols]
            ends[0, 2 * species + e, :, cols] = l0 * inverse[0, z, :, cols].astype(F32)
            ends[0, 2 * species + 2 + e, :, cols] = l1 * inverse[size - 1, z, :, cols].astype(F32)


def vertical(solved, low, high, before, after, inverse, link):
    species, blocks = solved.shape[:2]
    size, nz, ny, nx = inverse.shape
    count = nz // size
    tile = 16
    width = 2
    wide = width * LANES
    solved = solved.reshape(species, blocks, ny, nz, LANES)
    low = low.reshape(blocks, ny, nz, LANES)
    high = high.reshape(blocks, ny, nz, LANES)
    values = 2 * species + 4
    part_spec = pl.BlockSpec((species, size, tile, wide), lambda k, y, q: (0, k, y, q))
    side_spec = pl.BlockSpec((species, width, size, LANES), lambda k, y, q: (0, q, k, 0))
    spike_spec = pl.BlockSpec((width, tile, size, LANES), lambda k, y, q: (q, y, k, 0))
    return pl.pallas_call(
        vertical_kernel,
        grid=(count, ny // tile, blocks // width),
        out_shape=(
            jax.ShapeDtypeStruct((species, nz, ny, nx), F32),
            jax.ShapeDtypeStruct((count, values, ny, nx), F32),
        ),
        in_specs=[
            pl.BlockSpec((species, width, tile, size, LANES), lambda k, y, q: (0, q, y, k, 0)),
            spike_spec,
            spike_spec,
            side_spec,
            side_spec,
            pl.BlockSpec((size, size, tile, wide), lambda k, y, q: (0, k, y, q)),
            pl.BlockSpec((2, 1, tile, wide), lambda k, y, q: (0, k, y, q)),
        ],
        out_specs=(
            part_spec,
            pl.BlockSpec((1, values, tile, wide), lambda k, y, q: (k, 0, y, q)),
        ),
        scratch_shapes=[pltpu.VMEM((species, width, size * tile, LANES), F32)],
        compiler_params=pltpu.CompilerParams(vmem_limit_bytes=40 * 1024 * 1024),
        name="vertical",
    )(solved, low, high, before, after, inverse, link)


def chain(entries, species):
    offset = jnp.zeros_like(entries[0][:species])
    slope = jnp.zeros_like(entries[0][0])
    stored = []
    for item in entries:
        head, tail = item[:species], item[species : 2 * species]
        head_low, tail_low, head_high, tail_high = (item[2 * species + i] for i in range(4))
        factor = 1.0 / (1.0 - head_low * slope)
        base = (head + head_low * offset) * factor
        gain = head_high * factor
        stored.append((base, gain, offset, slope))
        offset = tail + tail_low * offset + tail_low * slope * base
        slope = tail_high + tail_low * slope * gain
    later = jnp.zeros_like(offset)
    results = []
    for base, gain, offset, slope in reversed(stored):
        here = base + gain * later
        results.append(jnp.concatenate([offset + slope * here, later], 0))
        later = here
    return results[::-1]


def local(conc, explicit_rate, x_coef, y_coef, z_inverse, z_link):
    species, nz, ny, nx = conc.shape
    values = 2 * species + 4
    solved, low, high, ends = horizontal(conc, explicit_rate, x_coef, y_coef)
    rows = lax.axis_size("row")
    blocks = ends.shape[1]
    cut = ends.reshape(values, blocks, rows, nz // rows, LANES)
    cut = jnp.moveaxis(cut, 2, 0)
    cut = lax.all_to_all(cut, "row", 0, 0)
    answer = jnp.stack(chain([cut[i] for i in range(rows)], species), 0)
    answer = lax.all_to_all(answer, "row", 0, 0)
    answer = jnp.moveaxis(answer, 0, 2).reshape(2 * species, blocks, nz, LANES)
    part, ends = vertical(
        solved, low, high, answer[:species], answer[species:], z_inverse, z_link
    )
    layers = lax.axis_size("layer")
    count = ends.shape[0]
    cut = ends.reshape(count, values, layers, ny // layers, nx)
    cut = jnp.moveaxis(cut, 2, 0)
    cut = lax.all_to_all(cut, "layer", 0, 0)
    answer = chain([cut[i, k] for i in range(layers) for k in range(count)], species)
    answer = jnp.stack(answer, 0).reshape(layers, count, 2 * species, ny // layers, nx)
    answer = lax.all_to_all(answer, "layer", 0, 0)
    answer = jnp.moveaxis(answer, 0, 2).reshape(count, 2 * species, ny, nx)
    size = z_inverse.shape[0]
    out = part.reshape(species, count, size, ny, nx)
    first = z_inverse[0].reshape(count, size, ny, nx).astype(F32)
    last = z_inverse[size - 1].reshape(count, size, ny, nx).astype(F32)
    below = jnp.moveaxis(answer[:, :species], 1, 0) * z_link[0][None]
    above = jnp.moveaxis(answer[:, species:], 1, 0) * z_link[1][None]
    out = out + first[None] * below[:, :, None] + last[None] * above[:, :, None]
    return out.reshape(conc.shape)


def solution(mesh):
    placed = P(None, "layer", "row", None)
    return jax.shard_map(
        local, mesh=mesh, in_specs=(placed,) * 6, out_specs=placed, check_vma=False
    )
```

time: 671 us -> 142 us (0.21); the launches traced: 658 us -> 142 us
  other arithmetic: 335 us -> 17.1 us
  local copies, waits for them, and re-layouts: 222 us -> 6.81 us
  waiting for transfers between devices: 74.8 us -> 10 us
  blocking collectives: 0 us -> 49.8 us
  Pallas kernels: 0 us -> 42.9 us
  between operations: 15.8 us -> 0.38 us
    mul x45 -> x5, other arithmetic: 167 us -> 0.31 us  [the longest x2 0.21 us: chain(): here = base + gain * later]
    slice x49 -> x5, local copies, waits for them, and re-layouts: 117 us -> 2.85 us  [the longest x2 2.78 us: neighbours(): first = lax.slice_in_dim(shard, 0, 1, axis=dim)]
    add x35 -> x17, other arithmetic: 81.2 us -> 8.04 us  [the longest x1 7.57 us: local(): out = out + first[None] * below[:, :, None] + last[None] * above[:, :, None]]
    all_gather x2 -> x0, waiting for transfers between devices: 70.6 us -> none  [the longest x1 41.9 us: local(): everyone = lax.all_gather(end_values[None], 'row', axis=0, tiled=True)]
    mul x56 -> x5, local copies, waits for them, and re-layouts: 61.4 us -> 3.09 us  [the longest x2 3.03 us: local(): out = out + first[None] * below[:, :, None] + last[None] * above[:, :, None]]
    dynamic_update_slice x48 -> x0, other arithmetic: 50.5 us -> none  [interface_solve(): lax.scan(forward, initial, (top_value, bottom_value, top_low, bottom_low,...]
    all_to_all x0 -> x3, blocking collectives: none -> 49.8 us  [the longest x1 20.9 us: local(): cut = lax.all_to_all(cut, 'row', 0, 0)]
    pallas_call x0 -> x2, Pallas kernels: none -> 42.9 us  [the longest x1 28.5 us: horizontal(): pl.pallas_call(horizontal_kernel, out_shape=(shape(species, *flat), shape...]
  transfers between devices with their start and end apart: 6 -> 5, of which waited for: 3 -> 3; matrix products, arithmetic and copies ran while one was open for 19% -> 4% of each run, Pallas kernels for 0% -> 0%
where the time goes in v1:
time: 142 us
  blocking collectives  49.8 us (35%)
  Pallas kernels  42.9 us (30%)
  other arithmetic  17.1 us (12%)
  starting transfers between devices  14.8 us (10%)
  waiting for transfers between devices  10 us (7%)
  local copies, waits for them, and re-layouts  6.81 us (5%)
    pallas_call x1, Pallas kernels, horizontal(): pl.pallas_call(horizontal_kernel, out_shape=(shape(species, *flat), shape...  28.5 us
    all_to_all x1, blocking collectives, local(): cut = lax.all_to_all(cut, 'row', 0, 0)  20.9 us
    all_to_all x1, blocking collectives, local(): cut = lax.all_to_all(cut, 'layer', 0, 0)  16.9 us
    pallas_call x1, Pallas kernels, vertical(): pl.pallas_call(vertical_kernel, grid=(count, ny // tile, blocks // width)...  14.4 us
    all_to_all x1, blocking collectives, local(): answer = lax.all_to_all(answer, 'row', 0, 0)  12 us
    ppermute x4, starting transfers between devices, neighbours(): return (lax.ppermute(last, axis, up), lax.ppermute(first, axis, down))  11.1 us
    add x1, other arithmetic, local(): out = out + first[None] * below[:, :, None] + last[None] * above[:, :, None]  7.57 us
    ppermute x4, waiting for transfers between devices, neighbours(): return (lax.ppermute(last, axis, up), lax.ppermute(first, axis, down))  5.6 us
  transfers between devices with their start and end apart: 5, of which 3 were waited for; matrix products, arithmetic and copies ran while one was open for 4% of the time, Pallas kernels for 0%

profile of v1, /device:TPU:0, one launch (start us, length us, event | category | flops | bytes accessed | tf_op | source)
XLA Modules:
  0.0 141.7 jit_solution(3446980992567868413)
XLA Ops:
  0.0 1.0 fusion.174
  1.0 1.3 collective-permute-start.1
  2.3 3.0 %collective-permute-start = (f32[2,1,32,512]{3,2,1,0:T(8,128)S(1)}, f32[2,1,32,512]{3,2,1,0:T(8,128)S(1)}, u32[]{:S(2)}, u32[]{:S(2)}) collective-permute-start(f32[2,1,32,512]{3,2,1,0:T(8,128)S(1)} %get-tuple-element.121), channel_id=1, source_target_pairs={{0,8},{8,16},{16,24},{1,9},{9,17},{17,25},{2,10},{10,18},{18,26},{... | collective-permute-start | bytes 393224 | tf_op jit(solution)/shard_map/ppermute | solution.py:21
  5.3 1.8 %fusion.173 = (f32[2,32,1,512]{3,2,1,0:T(1,128)S(1)}, f32[2,32,1,512]{3,2,1,0:T(1,128)S(1)}) fusion(f32[2,32,32,512]{3,2,1,0:T(8,128)} %conc.1), kind=kLoop, calls=%fused_computation.286 | loop fusion | bytes 524288 | tf_op jit(solution)/shard_map/slice | solution.py:20
  7.1 1.3 collective-permute-start.3
  8.4 5.5 %collective-permute-start.2 = (f32[2,32,1,512]{3,2,1,0:T(1,128)S(1)}, f32[2,32,1,512]{3,2,1,0:T(1,128)S(1)}, u32[]{:S(2)}, u32[]{:S(2)}) collective-permute-start(f32[2,32,1,512]{3,2,1,0:T(1,128)S(1)} %get-tuple-element.119), channel_id=1, source_target_pairs={{0,1},{1,2},{2,3},{3,4},{4,5},{5,6},{6,7},{8,9},{9,10},{10,11},{11... | collective-permute-start | bytes 393224 | tf_op jit(solution)/shard_map/ppermute | solution.py:21
  14.0 1.8 %collective-permute-done.3.yhi = f32[2,32,1,512]{3,2,1,0:T(1,128)S(1)} collective-permute-done((f32[2,32,1,512]{3,2,1,0:T(1,128)S(1)}, f32[2,32,1,512]{3,2,1,0:T(1,128)S(1)}, u32[]{:S(2)}, u32[]{:S(2)}) %collective-permute-start.3) | collective-permute-done | bytes 131104 | tf_op jit(solution)/shard_map/ppermute | solution.py:21
  15.8 3.8 %collective-permute-done.2.ylo = f32[2,32,1,512]{3,2,1,0:T(1,128)S(1)} collective-permute-done((f32[2,32,1,512]{3,2,1,0:T(1,128)S(1)}, f32[2,32,1,512]{3,2,1,0:T(1,128)S(1)}, u32[]{:S(2)}, u32[]{:S(2)}) %collective-permute-start.2) | collective-permute-done | bytes 131104 | tf_op jit(solution)/shard_map/ppermute | solution.py:21
  19.6 28.5 %horizontal.1 = (f32[2,4,1024,128]{3,2,1,0:T(8,128)}, f32[4,1024,128]{2,1,0:T(8,128)S(1)}, f32[4,1024,128]{2,1,0:T(8,128)}, f32[8,4,32,128]{3,2,1,0:T(8,128)S(1)}) custom-call(f32[2,32,32,512]{3,2,1,0:T(8,128)} %conc.1, f32[2,1,32,512]{3,2,1,0:T(8,128)S(1)} %collective-permute-done.zlo, f32[2,1,32,512]{3,2,1,0:T(8,128)S(1)} %collective-permute-done.1.zhi, ...), custom_call_target="tpu_custom_call" | custom-call | tf_op jit(solution)/shard_map/horizontal/pallas_call | solution.py:179
  48.1 0.1 copy.133
  48.2 20.9 %all_to_all.20 = f32[8,8,4,4,128]{4,3,2,1,0:T(4,128)S(1)} all-to-all(f32[8,8,4,4,128]{4,3,2,1,0:T(4,128)S(1)} %bitcast.687), channel_id=1, replica_groups=mesh['layer'=4,'row'=8] {'row'}, dimensions={0} | all-to-all | bytes 1048576 | tf_op jit(solution)/shard_map/all_to_all | solution.py:305
  69.1 0.1 fusion.90
  69.2 0.1 fusion.59
  69.7 12.0 %all_to_all.21 = f32[8,4,4,4,128]{4,3,2,1,0:T(4,128)S(1)} all-to-all(f32[8,4,4,4,128]{4,3,2,1,0:T(4,128)S(1)} %constant_dynamic-update-slice_fusion), channel_id=1, replica_groups=mesh['layer'=4,'row'=8] {'row'}, dimensions={0} | all-to-all | bytes 524288 | tf_op jit(solution)/shard_map/all_to_all | solution.py:307
  81.8 14.4 %vertical.1 = (f32[2,32,32,512]{3,2,1,0:T(8,128)S(1)}, f32[2,8,32,512]{3,2,1,0:T(8,128)S(1)}) custom-call(f32[2,4,32,32,128]{4,3,2,1,0:T(8,128)S(1)} %bitcast.679, f32[4,32,32,128]{3,2,1,0:T(8,128)S(1)} %bitcast.680, f32[4,32,32,128]{3,2,1,0:T(8,128)S(1)} %bitcast.681, f32[2,4,32,128]{3,2,1,0:T(8,128)S(1)} %bitcast.683, f32[2,4,32,128]{3,2,1,0:T(8,128)S(1)} %bitcast.682, ...), custom_call_target="tpu_custom_call" | custom-call | tf_op jit(solution)/shard_map/vertical/pallas_call | solution.py:249
  96.3 16.9 %all_to_all.22 = f32[4,2,8,8,512]{4,3,2,1,0:T(8,128)S(1)} all-to-all(f32[4,2,8,8,512]{4,3,2,1,0:T(8,128)S(1)} %copy_bitcast_fusion), channel_id=1, replica_groups=mesh['layer'=4,'row'=8] {'layer'}, dimensions={0} | all-to-all | bytes 2097152 | tf_op jit(solution)/shard_map/all_to_all | solution.py:316
  113.2 0.1 fusion.41
  113.3 0.1 fusion.10
  113.6 0.6 fusion.2
  114.2 0.6 fusion.3
  114.9 0.6 fusion.4
  115.5 0.6 fusion.5
  116.1 0.6 fusion.6
  116.8 0.6 fusion.7
  117.4 0.6 fusion.8
  118.0 0.6 bitcast_dynamic-update-slice_fusion
  118.6 3.6 %all-to-all-start.3 = ((f32[4,2,4,8,512]{4,3,2,1,0:T(8,128)}), f32[4,2,4,8,512]{4,3,2,1,0:T(8,128)S(1)}, u32[]{:S(2)}, u32[]{:S(2)}) async-start(f32[4,2,4,8,512]{4,3,2,1,0:T(8,128)} %bitcast.117), calls=%async_computation.3 | async-start | bytes 1048576 | tf_op jit(solution)/shard_map/all_to_all | solution.py:319
  122.3 4.1 %bitcast_convert_fusion.1 = (f32[32,32,512]{2,1,0:T(8,128)}, f32[32,32,512]{2,1,0:T(8,128)}) fusion(bf16[16,32,32,512]{3,2,1,0:T(8,128)(2,1)} %inverse.1), kind=kLoop, calls=%fused_computation.2 | loop fusion | flops 1048576 | bytes 6291456 | tf_op jit(solution)/shard_map/convert_element_type | solution.py:323
  126.5 4.5 %all-to-all-done.3 = f32[4,2,4,8,512]{4,3,2,1,0:T(8,128)S(1)} async-done(((f32[4,2,4,8,512]{4,3,2,1,0:T(8,128)}), f32[4,2,4,8,512]{4,3,2,1,0:T(8,128)S(1)}, u32[]{:S(2)}, u32[]{:S(2)}) %all-to-all-start.3) | async-done | bytes 524320 | tf_op jit(solution)/shard_map/all_to_all | solution.py:319
  131.1 0.5 mul.4073
  131.6 2.5 %mul.4065 = f32[2,2,16,32,512]{4,3,2,1,0:T(8,128)} broadcast(f32[2,2,32,512]{3,2,1,0:T(8,128)S(1)} %copy.128), dimensions={0,1,3,4} | broadcast | bytes 4456448 | tf_op jit(solution)/shard_map/mul | solution.py:327
  134.2 7.6 %multiply_add_fusion = f32[2,32,32,512]{3,2,1,0:T(8,128)} fusion(f32[2,32,32,512]{3,2,1,0:T(8,128)S(1)} %bitcast.685, f32[2,32,32,512]{3,2,1,0:T(8,128)S(1)} %copy-done.1, f32[2,32,32,512]{3,2,1,0:T(8,128)} %bitcast.686, f32[32,32,512]{2,1,0:T(8,128)} %get-tuple-element.117, f32[32,32,512]{2,1,0:T(8,128)} %get-tuple-element.116), kind=kLoop, calls=%fused_computation | loop fusion | flops 4194304 | bytes 20971520 | tf_op jit(solution)/shard_map/add | solution.py:327
  (48 shorter events, 0.8 us)
Async XLA Ops:
  1.0 13.0 %collective-permute-start.1 = (f32[2,1,32,512]{3,2,1,0:T(8,128)S(1)}, f32[2,1,32,512]{3,2,1,0:T(8,128)S(1)}, u32[]{:S(2)}, u32[]{:S(2)}) collective-permute-start(f32[2,1,32,512]{3,2,1,0:T(8,128)S(1)} %get-tuple-element.120), channel_id=1, source_target_pairs={{8,0},{16,8},{24,16},{9,1},{17,9},{25,17},{10,2},{18,10},{26,18},{... | collective-permute-start | bytes 393224 | tf_op jit(solution)/shard_map/ppermute | solution.py:21
  2.3 11.7 %collective-permute-start = (f32[2,1,32,512]{3,2,1,0:T(8,128)S(1)}, f32[2,1,32,512]{3,2,1,0:T(8,128)S(1)}, u32[]{:S(2)}, u32[]{:S(2)}) collective-permute-start(f32[2,1,32,512]{3,2,1,0:T(8,128)S(1)} %get-tuple-element.121), channel_id=1, source_target_pairs={{0,8},{8,16},{16,24},{1,9},{9,17},{17,25},{2,10},{10,18},{18,26},{... | collective-permute-start | bytes 393224 | tf_op jit(solution)/shard_map/ppermute | solution.py:21
  7.1 8.6 %collective-permute-start.3 = (f32[2,32,1,512]{3,2,1,0:T(1,128)S(1)}, f32[2,32,1,512]{3,2,1,0:T(1,128)S(1)}, u32[]{:S(2)}, u32[]{:S(2)}) collective-permute-start(f32[2,32,1,512]{3,2,1,0:T(1,128)S(1)} %get-tuple-element.118), channel_id=1, source_target_pairs={{1,0},{2,1},{3,2},{4,3},{5,4},{6,5},{7,6},{9,8},{10,9},{11,10},{12... | collective-permute-start | bytes 393224 | tf_op jit(solution)/shard_map/ppermute | solution.py:21
  8.4 11.1 %collective-permute-start.2 = (f32[2,32,1,512]{3,2,1,0:T(1,128)S(1)}, f32[2,32,1,512]{3,2,1,0:T(1,128)S(1)}, u32[]{:S(2)}, u32[]{:S(2)}) collective-permute-start(f32[2,32,1,512]{3,2,1,0:T(1,128)S(1)} %get-tuple-element.119), channel_id=1, source_target_pairs={{0,1},{1,2},{2,3},{3,4},{4,5},{5,6},{6,7},{8,9},{9,10},{10,11},{11... | collective-permute-start | bytes 393224 | tf_op jit(solution)/shard_map/ppermute | solution.py:21
  19.6 62.2 %copy-start.4 = (f32[2,2,32,512]{3,2,1,0:T(8,128)S(1)}, f32[2,2,32,512]{3,2,1,0:T(8,128)}, u32[]{:S(2)}) copy-start(f32[2,2,32,512]{3,2,1,0:T(8,128)} %link.1) | copy-start | bytes 786436
  48.1 33.7 %copy-start.2 = (f32[2,4,1024,128]{3,2,1,0:T(8,128)S(1)}, f32[2,4,1024,128]{3,2,1,0:T(8,128)}, u32[]{:S(2)}) copy-start(f32[2,4,1024,128]{3,2,1,0:T(8,128)} %get-tuple-element.11) | copy-start | bytes 12582916
  48.1 33.7 %copy-start.3 = (f32[4,1024,128]{2,1,0:T(8,128)S(1)}, f32[4,1024,128]{2,1,0:T(8,128)}, u32[]{:S(2)}) copy-start(f32[4,1024,128]{2,1,0:T(8,128)} %get-tuple-element.13) | copy-start | bytes 6291460
  96.2 17.4 %copy-start = (f32[2,32,32,512]{3,2,1,0:T(8,128)}, f32[2,32,32,512]{3,2,1,0:T(8,128)S(1)}, u32[]{:S(2)}) copy-start(f32[2,32,32,512]{3,2,1,0:T(8,128)S(1)} %get-tuple-element.15) | copy-start | bytes 12582916
  118.6 12.3 %all-to-all-start.3 = ((f32[4,2,4,8,512]{4,3,2,1,0:T(8,128)}), f32[4,2,4,8,512]{4,3,2,1,0:T(8,128)S(1)}, u32[]{:S(2)}, u32[]{:S(2)}) async-start(f32[4,2,4,8,512]{4,3,2,1,0:T(8,128)} %bitcast.117), calls=%async_computation.3 | async-start | bytes 1048576 | tf_op jit(solution)/shard_map/all_to_all | solution.py:319
  131.1 3.1 %copy-start.1 = (f32[2,32,32,512]{3,2,1,0:T(8,128)S(1)}, f32[2,32,32,512]{3,2,1,0:T(8,128)}, u32[]{:S(2)}) copy-start(f32[2,32,32,512]{3,2,1,0:T(8,128)} %copy-done) | copy-start | bytes 12582916

commit v2 on v1

--- a/solution.py
+++ b/solution.py
@@ -294,6 +294,75 @@
     return results[::-1]
 
 
+def exchange_kernel(axis, species, count, cut, final, inbox, answer, send, recv, send_back, recv_back):
+    parts, _, rows, wide = cut.shape
+    values = 2 * species + 4
+    me = lax.axis_index(axis)
+    mesh_id = pl.DeviceIdType.MESH
+    peers = [lax.rem(me + d, parts) for d in range(1, parts)]
+    barrier = pltpu.get_barrier_semaphore()
+    for peer in peers:
+        pl.semaphore_signal(barrier, inc=1, device_id={axis: peer}, device_id_type=mesh_id)
+    pl.semaphore_wait(barrier, parts - 1)
+
+    def copies(source, target, out_sem, in_sem):
+        made = [
+            pltpu.make_async_remote_copy(
+                src_ref=source.at[peer],
+                dst_ref=target.at[me],
+                send_sem=out_sem.at[d],
+                recv_sem=in_sem.at[d],
+                device_id={axis: peer},
+                device_id_type=mesh_id,
+            )
+            for d, peer in enumerate(peers)
+        ]
+        for copy in made:
+            copy.start()
+        return made
+
+    there = copies(cut, inbox, send, recv)
+    inbox[me] = cut[me]
+    for copy in there:
+        copy.wait_recv()
+    step = min(rows, SUB)
+    for t in range(rows // step):
+        for c in range(wide // LANES):
+            at = (slice(t * step, (t + 1) * step), slice(c * LANES, (c + 1) * LANES))
+            entries = [
+                inbox[i, k * values : (k + 1) * values, at[0], at[1]]
+                for i in range(parts)
+                for k in range(count)
+            ]
+            for n, result in enumerate(chain(entries, species)):
+                i, k = divmod(n, count)
+                answer[i, 2 * species * k : 2 * species * (k + 1), at[0], at[1]] = result
+    back = copies(answer, final, send_back, recv_back)
+    final[me] = answer[me]
+    for copy in there:
+        copy.wait_send()
+    for copy in back:
+        copy.wait()
+
+
+def exchange(cut, axis, species, count, number):
+    parts, _, rows, wide = cut.shape
+    vmem = pl.BlockSpec(memory_space=pltpu.VMEM)
+    reply = (parts, 2 * species * count, rows, wide)
+    return pl.pallas_call(
+        functools.partial(exchange_kernel, axis, species, count),
+        out_shape=jax.ShapeDtypeStruct(reply, F32),
+        in_specs=[vmem],
+        out_specs=vmem,
+        scratch_shapes=[pltpu.VMEM(cut.shape, F32), pltpu.VMEM(reply, F32)]
+        + [pltpu.SemaphoreType.DMA((parts - 1,))] * 4,
+        compiler_params=pltpu.CompilerParams(
+            collective_id=number, has_side_effects=True, vmem_limit_bytes=24 * 1024 * 1024
+        ),
+        name="exchange_" + axis,
+    )(cut)
+
+
 def local(conc, explicit_rate, x_coef, y_coef, z_inverse, z_link):
     species, nz, ny, nx = conc.shape
     values = 2 * species + 4
@@ -301,10 +370,9 @@
     rows = lax.axis_size("row")
     blocks = ends.shape[1]
     cut = ends.reshape(values, blocks, rows, nz // rows, LANES)
-    cut = jnp.moveaxis(cut, 2, 0)
-    cut = lax.all_to_all(cut, "row", 0, 0)
-    answer = jnp.stack(chain([cut[i] for i in range(rows)], species), 0)
-    answer = lax.all_to_all(answer, "row", 0, 0)
+    cut = jnp.moveaxis(cut, 2, 0).reshape(rows, values, -1, LANES)
+    answer = exchange(cut, "row", species, 1, 0)
+    answer = answer.reshape(rows, 2 * species, blocks, nz // rows, LANES)
     answer = jnp.moveaxis(answer, 0, 2).reshape(2 * species, blocks, nz, LANES)
     part, ends = vertical(
         solved, low, high, answer[:species], answer[species:], z_inverse, z_link
@@ -312,11 +380,9 @@
     layers = lax.axis_size("layer")
     count = ends.shape[0]
     cut = ends.reshape(count, values, layers, ny // layers, nx)
-    cut = jnp.moveaxis(cut, 2, 0)
-    cut = lax.all_to_all(cut, "layer", 0, 0)
-    answer = chain([cut[i, k] for i in range(layers) for k in range(count)], species)
-    answer = jnp.stack(answer, 0).reshape(layers, count, 2 * species, ny // layers, nx)
-    answer = lax.all_to_all(answer, "layer", 0, 0)
+    cut = jnp.moveaxis(cut, 2, 0).reshape(layers, count * values, ny // layers, nx)
+    answer = exchange(cut, "layer", species, count, 1)
+    answer = answer.reshape(layers, count, 2 * species, ny // layers, nx)
     answer = jnp.moveaxis(answer, 0, 2).reshape(count, 2 * species, ny, nx)
     size = z_inverse.shape[0]
     out = part.reshape(species, count, size, ny, nx)

time: 142 us -> 120 us (0.85)
  blocking collectives: 49.8 us -> 0 us
  Pallas kernels: 42.9 us -> 86.2 us
  waiting for transfers between devices: 10 us -> 1.49 us
  other arithmetic: 17.1 us -> 11.7 us
  starting transfers between devices: 14.8 us -> 11.1 us
  local copies, waits for them, and re-layouts: 6.81 us -> 8.44 us
    all_to_all x3 -> x0, blocking collectives: 49.8 us -> none  [the longest x1 20.9 us: local(): cut = lax.all_to_all(cut, 'row', 0, 0)]
    pallas_call x0 -> x2, Pallas kernels: none -> 43.2 us  [exchange(): pl.pallas_call(functools.partial(exchange_kernel, axis, species, count),...]
    unnamed x14 -> x0, other arithmetic: 4.51 us -> none
    all_to_all x1 -> x0, waiting for transfers between devices: 4.45 us -> none  [local(): answer = lax.all_to_all(answer, 'layer', 0, 0)]
    ppermute x4, waiting for transfers between devices: 5.6 us -> 1.49 us  [neighbours(): return (lax.ppermute(last, axis, up), lax.ppermute(first, axis, down))]
    all_to_all x1 -> x0, starting transfers between devices: 3.65 us -> none  [local(): answer = lax.all_to_all(answer, 'layer', 0, 0)]
    unnamed x10 -> x6, local copies, waits for them, and re-layouts: 0.02 us -> 2.19 us
  transfers between devices with their start and end apart: 5 -> 4, of which waited for: 3 -> 1; matrix products, arithmetic and copies ran while one was open for 4% -> 5% of each run, Pallas kernels for 0% -> 0%
where the time goes in v2:
time: 120 us; the launch traced here: 119 us
  Pallas kernels  86.2 us (72%)
  other arithmetic  11.7 us (10%)
  starting transfers between devices  11.1 us (9%)
  local copies, waits for them, and re-layouts  8.44 us (7%)
  waiting for transfers between devices  1.49 us (1%)
    pallas_call x2, Pallas kernels, exchange(): pl.pallas_call(functools.partial(exchange_kernel, axis, species, count),...  43.2 us
    pallas_call x1, Pallas kernels, horizontal(): pl.pallas_call(horizontal_kernel, out_shape=(shape(species, *flat), shape...  28.6 us
    pallas_call x1, Pallas kernels, vertical(): pl.pallas_call(vertical_kernel, grid=(count, ny // tile, blocks // width)...  14.3 us
    ppermute x4, starting transfers between devices, neighbours(): return (lax.ppermute(last, axis, up), lax.ppermute(first, axis, down))  11.1 us
    add x1, other arithmetic, local(): out = out + first[None] * below[:, :, None] + last[None] * above[:, :, None]  7.57 us
    convert_element_type x1, other arithmetic, local(): first = z_inverse[0].reshape(count, size, ny, nx).astype(F32)  4.08 us
    mul x2, local copies, waits for them, and re-layouts, local(): out = out + first[None] * below[:, :, None] + last[None] * above[:, :, None]  3.08 us
    slice x2, local copies, waits for them, and re-layouts, neighbours(): first = lax.slice_in_dim(shard, 0, 1, axis=dim)  2.82 us
  transfers between devices with their start and end apart: 4, of which 1 were waited for; matrix products, arithmetic and copies ran while one was open for 5% of the time, Pallas kernels for 0%

profile of v2, /device:TPU:0, one launch (start us, length us, event | category | flops | bytes accessed | tf_op | source)
XLA Modules:
  0.0 119.1 jit_solution(10370805824573855944)
XLA Ops:
  0.0 0.0 copy-start.2
  0.0 1.0 fusion.3
  1.0 1.3 %collective-permute-start.1 = (f32[2,1,32,512]{3,2,1,0:T(8,128)S(1)}, f32[2,1,32,512]{3,2,1,0:T(8,128)S(1)}, u32[]{:S(2)}, u32[]{:S(2)}) collective-permute-start(f32[2,1,32,512]{3,2,1,0:T(8,128)S(1)} %get-tuple-element.21), channel_id=1, source_target_pairs={{8,0},{16,8},{24,16},{9,1},{17,9},{25,17},{10,2},{18,10},{26,18},{... | collective-permute-start | bytes 393224 | tf_op jit(solution)/shard_map/ppermute | solution.py:21
  2.3 3.0 %collective-permute-start = (f32[2,1,32,512]{3,2,1,0:T(8,128)S(1)}, f32[2,1,32,512]{3,2,1,0:T(8,128)S(1)}, u32[]{:S(2)}, u32[]{:S(2)}) collective-permute-start(f32[2,1,32,512]{3,2,1,0:T(8,128)S(1)} %get-tuple-element.22), channel_id=1, source_target_pairs={{0,8},{8,16},{16,24},{1,9},{9,17},{17,25},{2,10},{10,18},{18,26},{... | collective-permute-start | bytes 393224 | tf_op jit(solution)/shard_map/ppermute | solution.py:21
  5.4 1.8 %fusion.2 = (f32[2,32,1,512]{3,2,1,0:T(1,128)S(1)}, f32[2,32,1,512]{3,2,1,0:T(1,128)S(1)}) fusion(f32[2,32,32,512]{3,2,1,0:T(8,128)} %conc.1), kind=kLoop, calls=%fused_computation.11 | loop fusion | bytes 524288 | tf_op jit(solution)/shard_map/slice | solution.py:20
  7.2 1.3 %collective-permute-start.3 = (f32[2,32,1,512]{3,2,1,0:T(1,128)S(1)}, f32[2,32,1,512]{3,2,1,0:T(1,128)S(1)}, u32[]{:S(2)}, u32[]{:S(2)}) collective-permute-start(f32[2,32,1,512]{3,2,1,0:T(1,128)S(1)} %get-tuple-element.19), channel_id=1, source_target_pairs={{1,0},{2,1},{3,2},{4,3},{5,4},{6,5},{7,6},{9,8},{10,9},{11,10},{12... | collective-permute-start | bytes 393224 | tf_op jit(solution)/shard_map/ppermute | solution.py:21
  8.5 5.5 %collective-permute-start.2 = (f32[2,32,1,512]{3,2,1,0:T(1,128)S(1)}, f32[2,32,1,512]{3,2,1,0:T(1,128)S(1)}, u32[]{:S(2)}, u32[]{:S(2)}) collective-permute-start(f32[2,32,1,512]{3,2,1,0:T(1,128)S(1)} %get-tuple-element.20), channel_id=1, source_target_pairs={{0,1},{1,2},{2,3},{3,4},{4,5},{5,6},{6,7},{8,9},{9,10},{10,11},{11... | collective-permute-start | bytes 393224 | tf_op jit(solution)/shard_map/ppermute | solution.py:21
  14.0 4.1 %bitcast_convert_fusion.1 = (f32[32,32,512]{2,1,0:T(8,128)}, f32[32,32,512]{2,1,0:T(8,128)}) fusion(bf16[16,32,32,512]{3,2,1,0:T(8,128)(2,1)} %inverse.1), kind=kLoop, calls=%fused_computation.2 | loop fusion | flops 1048576 | bytes 6291456 | tf_op jit(solution)/shard_map/convert_element_type | solution.py:389
  18.1 0.0 copy-done.2
  18.1 0.0 collective-permute-done.1.zhi
  18.1 0.0 collective-permute-done.zlo
  18.1 0.0 collective-permute-done.3.yhi
  18.1 1.5 %collective-permute-done.2.ylo = f32[2,32,1,512]{3,2,1,0:T(1,128)S(1)} collective-permute-done((f32[2,32,1,512]{3,2,1,0:T(1,128)S(1)}, f32[2,32,1,512]{3,2,1,0:T(1,128)S(1)}, u32[]{:S(2)}, u32[]{:S(2)}) %collective-permute-start.2) | collective-permute-done | bytes 131104 | tf_op jit(solution)/shard_map/ppermute | solution.py:21
  19.6 28.6 %horizontal.1 = (f32[2,4,1024,128]{3,2,1,0:T(8,128)}, f32[4,1024,128]{2,1,0:T(8,128)S(1)}, f32[4,1024,128]{2,1,0:T(8,128)}, f32[8,4,32,128]{3,2,1,0:T(8,128)S(1)}) custom-call(f32[2,32,32,512]{3,2,1,0:T(8,128)} %conc.1, f32[2,1,32,512]{3,2,1,0:T(8,128)S(1)} %collective-permute-done.zlo, f32[2,1,32,512]{3,2,1,0:T(8,128)S(1)} %collective-permute-done.1.zhi, ...), custom_call_target="tpu_custom_call" | custom-call | tf_op jit(solution)/shard_map/horizontal/pallas_call | solution.py:179
  48.2 0.0 copy-start.1
  48.2 0.1 copy.10
  48.3 23.9 %exchange_row.1 = f32[8,4,16,128]{3,2,1,0:T(8,128)S(1)} custom-call(f32[8,8,16,128]{3,2,1,0:T(8,128)S(1)} %bitcast.44), custom_call_target="tpu_custom_call" | custom-call | tf_op jit(solution)/shard_map/exchange_row/pallas_call | solution.py:352
  72.2 0.1 copy.19
  72.3 0.0 copy-done.1
  72.4 0.0 copy-start
  72.4 2.2 %copy-done = f32[2,4,1024,128]{3,2,1,0:T(8,128)S(1)} copy-done((f32[2,4,1024,128]{3,2,1,0:T(8,128)S(1)}, f32[2,4,1024,128]{3,2,1,0:T(8,128)}, u32[]{:S(2)}) %copy-start) | copy-done | bytes 4194328
  74.5 14.3 %vertical.1 = (f32[2,32,32,512]{3,2,1,0:T(8,128)S(1)}, f32[2,8,32,512]{3,2,1,0:T(8,128)S(1)}) custom-call(f32[2,4,32,32,128]{4,3,2,1,0:T(8,128)S(1)} %bitcast.39, f32[4,32,32,128]{3,2,1,0:T(8,128)S(1)} %bitcast.41, f32[4,32,32,128]{3,2,1,0:T(8,128)S(1)} %bitcast.42, f32[2,4,32,128]{3,2,1,0:T(8,128)S(1)} %bitcast.48, f32[2,4,32,128]{3,2,1,0:T(8,128)S(1)} %bitcast.47, ...), custom_call_target="tpu_custom_call" | custom-call | tf_op jit(solution)/shard_map/vertical/pallas_call | solution.py:249
  88.9 0.1 copy.12
  89.0 19.3 %exchange_layer.1 = f32[4,8,8,512]{3,2,1,0:T(8,128)S(1)} custom-call(f32[4,16,8,512]{3,2,1,0:T(8,128)S(1)} %bitcast.40), custom_call_target="tpu_custom_call" | custom-call | tf_op jit(solution)/shard_map/exchange_layer/pallas_call | solution.py:352
  108.3 0.1 fusion.1
  108.5 0.5 mul.71
  109.0 2.6 %mul.63 = f32[2,2,16,32,512]{4,3,2,1,0:T(8,128)} broadcast(f32[2,2,32,512]{3,2,1,0:T(8,128)S(1)} %copy.14), dimensions={0,1,3,4} | broadcast | bytes 4456448 | tf_op jit(solution)/shard_map/mul | solution.py:393
  111.5 7.6 %multiply_add_fusion = f32[2,32,32,512]{3,2,1,0:T(8,128)} fusion(f32[2,32,32,512]{3,2,1,0:T(8,128)S(1)} %bitcast.50, f32[2,32,32,512]{3,2,1,0:T(8,128)S(1)} %get-tuple-element.15, f32[2,32,32,512]{3,2,1,0:T(8,128)} %bitcast.51, f32[32,32,512]{2,1,0:T(8,128)} %get-tuple-element.18, f32[32,32,512]{2,1,0:T(8,128)} %get-tuple-element.17), kind=kLoop, calls=%fused_computation | loop fusion | flops 4194304 | bytes 20971520 | tf_op jit(solution)/shard_map/add | solution.py:393
  (5 shorter events, 0.1 us)
Async XLA Ops:
  0.0 18.1 %copy-start.2 = (f32[2,2,32,512]{3,2,1,0:T(8,128)S(1)}, f32[2,2,32,512]{3,2,1,0:T(8,128)}, u32[]{:S(2)}) copy-start(f32[2,2,32,512]{3,2,1,0:T(8,128)} %link.1) | copy-start | bytes 786436
  1.0 17.1 %collective-permute-start.1 = (f32[2,1,32,512]{3,2,1,0:T(8,128)S(1)}, f32[2,1,32,512]{3,2,1,0:T(8,128)S(1)}, u32[]{:S(2)}, u32[]{:S(2)}) collective-permute-start(f32[2,1,32,512]{3,2,1,0:T(8,128)S(1)} %get-tuple-element.21), channel_id=1, source_target_pairs={{8,0},{16,8},{24,16},{9,1},{17,9},{25,17},{10,2},{18,10},{26,18},{... | collective-permute-start | bytes 393224 | tf_op jit(solution)/shard_map/ppermute | solution.py:21
  2.3 15.8 %collective-permute-start = (f32[2,1,32,512]{3,2,1,0:T(8,128)S(1)}, f32[2,1,32,512]{3,2,1,0:T(8,128)S(1)}, u32[]{:S(2)}, u32[]{:S(2)}) collective-permute-start(f32[2,1,32,512]{3,2,1,0:T(8,128)S(1)} %get-tuple-element.22), channel_id=1, source_target_pairs={{0,8},{8,16},{16,24},{1,9},{9,17},{17,25},{2,10},{10,18},{18,26},{... | collective-permute-start | bytes 393224 | tf_op jit(solution)/shard_map/ppermute | solution.py:21
  7.2 10.9 %collective-permute-start.3 = (f32[2,32,1,512]{3,2,1,0:T(1,128)S(1)}, f32[2,32,1,512]{3,2,1,0:T(1,128)S(1)}, u32[]{:S(2)}, u32[]{:S(2)}) collective-permute-start(f32[2,32,1,512]{3,2,1,0:T(1,128)S(1)} %get-tuple-element.19), channel_id=1, source_target_pairs={{1,0},{2,1},{3,2},{4,3},{5,4},{6,5},{7,6},{9,8},{10,9},{11,10},{12... | collective-permute-start | bytes 393224 | tf_op jit(solution)/shard_map/ppermute | solution.py:21
  8.5 11.1 %collective-permute-start.2 = (f32[2,32,1,512]{3,2,1,0:T(1,128)S(1)}, f32[2,32,1,512]{3,2,1,0:T(1,128)S(1)}, u32[]{:S(2)}, u32[]{:S(2)}) collective-permute-start(f32[2,32,1,512]{3,2,1,0:T(1,128)S(1)} %get-tuple-element.20), channel_id=1, source_target_pairs={{0,1},{1,2},{2,3},{3,4},{4,5},{5,6},{6,7},{8,9},{9,10},{10,11},{11... | collective-permute-start | bytes 393224 | tf_op jit(solution)/shard_map/ppermute | solution.py:21
  48.2 24.1 %copy-start.1 = (f32[4,1024,128]{2,1,0:T(8,128)S(1)}, f32[4,1024,128]{2,1,0:T(8,128)}, u32[]{:S(2)}) copy-start(f32[4,1024,128]{2,1,0:T(8,128)} %get-tuple-element.13) | copy-start | bytes 6291460
  72.4 2.2 %copy-start = (f32[2,4,1024,128]{3,2,1,0:T(8,128)S(1)}, f32[2,4,1024,128]{3,2,1,0:T(8,128)}, u32[]{:S(2)}) copy-start(f32[2,4,1024,128]{3,2,1,0:T(8,128)} %get-tuple-element.11) | copy-start | bytes 12582916
